TPU v7x, 256 devices: a whole 4x4x8 slice. The times are simulated.
256 devices in a mesh: comp: 128 (over x, y, z), blk: 2 (over core).
Axes of the slice: x: 4, y: 4, z: 8, core: 2. Of those that a mesh axis runs over, the one named last changes fastest.
Arguments:
- constraint_modes: bfloat16 [128, 2048, 1024], P('comp', 'blk'), may hold values from -6 to 6
- stiff_blocks: bfloat16 [128, 2048, 512], P('comp', 'blk'), may hold values from -0.25 to 0.25
- block_cols: int32 [128, 32, 8], P('comp', 'blk'), may hold values from 0 to 31, as said below
- flange_rows: int32 [128, 252], P('comp', 'blk'), may hold values from 0 to 1023, as said below
- flange_dest: int32 [128, 252], P('comp', 'blk'), may hold values from 0 to 127, as said below
- flange_match: int32 [128, 252], P('comp', 'blk'), may hold values from 0 to 251, as said below
- flange_stiff: float32 [128, 252], P('comp', 'blk'), may hold values from 0.3 to 3
- joint_rows: int32 [128, 512], P('comp', 'blk'), may hold values from 0 to 1023
- joint_owner: int32 [128, 512], P('comp', 'blk'), may hold values from 0 to 127, as said below
- joint_local: int32 [128, 512], P('comp', 'blk'), may hold values from 0 to 63
Outputs:
- reduced_stiff: float32 [128, 1024, 1024], P('comp', None, 'blk')
- joint_forces: float32 [8192, 1024], P('comp', 'blk')
Inputs may be any that keep to these rules, and one draw needn't show every extreme that they name: `block_cols`: the 8 block columns of one block row are different. `flange_rows`: the flange rows of one half of a component are different rows of that half. `flange_dest`: within each half of a component the entries form 63 groups of 2 consecutive entries; all entries of a group pair with the entries of one group of one other component in the same half, and the groups of one half pair with different components. `flange_match`: the pairing is mutual: if entry n of c names entry m of p, then entry m of p names entry n of c. `joint_owner`: at most 4 of the 256 entries of one half of a component name one owner, and one owner is named exactly 4 times by every half of every component.
All inputs are finite; a program needn't handle non-finite values.
Results may differ from a plain program's by a relative error of at most 0.0028.
Values may be sent and summed in bfloat16 or wider, within the bound.
A program may use at most 128 MiB of HBM per device.

v0:
```python
import math

import jax
import jax.numpy as jnp
from jax import lax
from jax.experimental import pallas as pl
from jax.experimental.pallas import tpu as pltpu
from jax.sharding import PartitionSpec as P

MESH = pl.DeviceIdType.MESH
BLOCK = 64
NEIGH = 8
FCAP = 2
JCAP = 4
JOWN = 64
NZ = 8
LANES = 128
f32 = jnp.float32
bf16 = jnp.bfloat16


def iota(shape, dim):
    return lax.broadcasted_iota(jnp.int32, shape, dim).astype(f32)


def ones_where(mask):
    return jnp.where(mask, 1.0, 0.0).astype(bf16)


def dot(left, right):
    return jnp.dot(left, right, preferred_element_type=f32)


def as_column(row):
    n = row.shape[1]
    return jnp.sum(jnp.where(iota((n, n), 0) == iota((n, n), 1), row, 0.0), axis=1, keepdims=True)


def kernel(
    modes_hbm, stiff_hbm, block_cols, flange_rows, flange_dest, flange_match, flange_stiff,
    joint_rows, joint_owner, joint_local,
    reduced_hbm, forces,
    whole, stiff, vec, flange_send, flange_recv, relay, incoming, base, high, low,
    bolt, select_row, joint_select, joint_flange, joint_bolt, joint_base,
    id_send, id_recv, place, rows_send, rows_recv, round_send, round_full,
    part_send, part_recv, reduced,
    load_sem, flange_sem, modes_sem, id_sem, rows_send_sem, rows_recv_sem,
    round_sem, part_send_sem, part_recv_sem, out_sem,
):
    ncomp = lax.axis_size("comp")
    nplane = ncomp // NZ
    comp = lax.axis_index("comp")
    half = lax.axis_index("blk")
    other = 1 - half
    plane = comp // NZ
    zpos = lax.rem(comp, NZ)
    rows, iface = stiff.shape[0], whole.shape[2]
    cols = iface // 2
    nflange = flange_rows.shape[1]
    fslots = ncomp * FCAP
    jslots = ncomp * JCAP
    chunks = iface // LANES
    quarter = chunks // 2
    own_rows = pl.ds(pl.multiple_of(half * rows, rows), rows)
    nblocks = rows // BLOCK
    own_blocks = pl.ds(half * nblocks, nblocks)
    here = half * nplane + plane

    def to(c, b):
        return dict(device_id={"comp": c, "blk": b}, device_id_type=MESH)

    load_modes = pltpu.make_async_copy(modes_hbm, whole.at[own_blocks], load_sem.at[0])
    load_stiff = pltpu.make_async_copy(stiff_hbm.at[0], stiff, load_sem.at[1])
    load_modes.start()
    load_stiff.start()

    barrier = pltpu.get_barrier_semaphore()

    def greet(k, carry):
        pl.semaphore_signal(barrier, inc=1, **to(lax.rem(comp + k, ncomp), half))
        return carry

    def greet_plane(k, carry):
        pl.semaphore_signal(barrier, inc=1, **to(k * NZ + zpos, other))
        return carry

    lax.fori_loop(1, ncomp, greet, 0)
    lax.fori_loop(0, nplane, greet_plane, 0)

    vec[...] = jnp.full(vec.shape, -1.0, f32)
    parity = lax.broadcasted_iota(jnp.int32, (1, nflange), 1) & 1
    vec[0:1, 0:nflange] = flange_rows[...].astype(f32)
    vec[1:2, 0:nflange] = (flange_dest[...] * FCAP + parity).astype(f32)
    vec[2:3, 0:nflange] = (flange_dest[...] * FCAP + (flange_match[...] & 1)).astype(f32)
    vec[3:4, 0:nflange] = flange_stiff[...]
    frow, out_slot, in_slot, fstiff = vec[0:1, :], vec[1:2, :], vec[2:3, :], vec[3:4, :]
    row_of_slot = jnp.sum(
        jnp.where(iota((fslots, LANES), 0) == out_slot, frow + 1.0, 0.0), axis=1, keepdims=True
    ) - 1.0
    pick = ones_where(row_of_slot == iota((fslots, rows), 1))
    load_modes.wait()
    for j in range(0, chunks, 2):
        got = dot(pick, whole[own_blocks, :, j * LANES : (j + 2) * LANES].reshape(rows, 2 * LANES))
        relay[pl.ds(j, fslots, stride=chunks), :] = got[:, :LANES]
        relay[pl.ds(j + 1, fslots, stride=chunks), :] = got[:, LANES:]
    flange_send[...] = relay[...].astype(bf16)
    flange_recv[pl.ds(pl.multiple_of(comp * 16, 16), 16), :] = jnp.zeros((16, LANES), bf16)

    pl.semaphore_wait(barrier, ncomp - 1 + nplane)

    def flange_copy(k):
        dest = lax.rem(comp + k, ncomp)
        return pltpu.make_async_remote_copy(
            flange_send.at[pl.ds(pl.multiple_of(dest * 16, 16), 16)],
            flange_recv.at[pl.ds(pl.multiple_of(comp * 16, 16), 16)],
            flange_sem.at[0], flange_sem.at[1], **to(dest, half),
        )

    def send_flange(k, carry):
        flange_copy(k).start()
        return carry

    lax.fori_loop(1, ncomp, send_flange, 0)

    modes_copy = pltpu.make_async_remote_copy(
        whole.at[own_blocks], whole.at[own_blocks], modes_sem.at[0], modes_sem.at[1], **to(comp, other)
    )
    modes_copy.start()

    owner = joint_owner[...].astype(f32)
    local = joint_local[...].astype(f32)
    njoint = owner.shape[1]
    square = (njoint, njoint)
    before = (as_column(owner) == owner) & (iota(square, 0) < iota(square, 1))
    position = jnp.sum(jnp.where(before, 1.0, 0.0), axis=0, keepdims=True)
    jslot = owner * JCAP + position
    group = NZ * JCAP
    jslot_int = jslot.astype(jnp.int32)
    lane = (jslot_int & (group - 1)) + (plane & 3) * group
    of_plane = ones_where(
        lax.broadcasted_iota(jnp.int32, (nplane, njoint), 0) == (joint_owner[...] // NZ)
    )
    at_lane = jnp.where(
        lax.broadcasted_iota(jnp.int32, (LANES, njoint), 0) == lane, local + 1.0, 0.0
    ).astype(bf16)
    ids = lax.dot_general(of_plane, at_lane, (((1,), (1,)), ((), ())), preferred_element_type=f32)
    for d in range(nplane):
        id_send[d] = ids[d : d + 1, :]
    id_recv[pl.ds(here, 1)] = id_send[pl.ds(plane, 1)]

    def id_copy(k, b):
        dest = lax.rem(plane + k, nplane)
        return pltpu.make_async_remote_copy(
            id_send.at[pl.ds(dest, 1)], id_recv.at[pl.ds(here, 1)],
            id_sem.at[0], id_sem.at[1], **to(dest * NZ + zpos, b),
        )

    def send_ids(k, carry):
        id_copy(k, half).start()
        id_copy(k, other).start()
        return carry

    id_copy(0, other).start()
    lax.fori_loop(1, nplane, send_ids, 0)

    at_row = iota((rows, LANES), 0) == frow
    slot_of_row = jnp.sum(jnp.where(at_row, in_slot + 1.0, 0.0), axis=1, keepdims=True) - 1.0
    bolt[...] = jnp.broadcast_to(
        jnp.sum(jnp.where(at_row, fstiff, 0.0), axis=1, keepdims=True), bolt.shape
    )
    select_row[...] = ones_where(slot_of_row == iota((rows, fslots), 1))
    by_row = as_column(frow) == iota((LANES, rows), 1)
    slots_along = jnp.sum(jnp.where(by_row, as_column(in_slot) + 1.0, 0.0), axis=0, keepdims=True)
    bolts_along = jnp.sum(jnp.where(by_row, as_column(fstiff), 0.0), axis=0, keepdims=True)
    joint_row = jnp.sum(
        jnp.where(iota((jslots, njoint), 0) == jslot, joint_rows[...].astype(f32) + 1.0, 0.0),
        axis=1, keepdims=True,
    ) - 1.0
    takes = joint_row == iota((jslots, rows), 1)
    joint_select[...] = ones_where(takes)
    joint_slot = jnp.sum(jnp.where(takes, slots_along, 0.0), axis=1, keepdims=True) - 1.0
    joint_flange[...] = ones_where(joint_slot == iota((jslots, fslots), 1))
    joint_bolt[...] = jnp.broadcast_to(
        jnp.sum(jnp.where(takes, bolts_along, 0.0), axis=1, keepdims=True), joint_bolt.shape
    )

    load_stiff.wait()
    modes_copy.wait()

    def block_row(r, carry):
        at = pl.ds(pl.multiple_of(r * BLOCK, BLOCK), BLOCK)
        taken = jnp.concatenate(
            [
                whole[block_cols[0, r, k]]
                for k in range(NEIGH)
            ],
            axis=0,
        )
        own = whole[half * nblocks + r].astype(f32)
        value = dot(stiff[at, :], taken) + bolt[at, 0:1] * own
        top = value.astype(bf16)
        rest = (value - top.astype(f32)).astype(bf16)
        for e in range(2):
            here_cols = slice(e * cols, (e + 1) * cols)
            base[e, at, :] = value[:, here_cols]
            high[e, at, :] = top[:, here_cols]
            low[e, at, :] = rest[:, here_cols]
        return carry

    lax.fori_loop(0, rows // BLOCK, block_row, 0)
    for e in range(2):
        joint_base[e] = dot(joint_select[...], high[e]) + dot(joint_select[...], low[e])

    id_all = id_recv.at[pl.ds(0, 2 * nplane - 1)]
    id_wait = pltpu.make_async_remote_copy(
        id_all, id_all, id_sem.at[0], id_sem.at[1], **to(comp, other)
    )
    id_wait.wait_recv()
    lane_z = ((lax.broadcasted_iota(jnp.int32, (1, LANES), 1) & (group - 1)) // JCAP).astype(f32)
    for g in range(2 * nplane // 4):
        four = id_recv[4 * g] + id_recv[4 * g + 1] + id_recv[4 * g + 2] + id_recv[4 * g + 3]
        key = jnp.where(four > 0.5, lane_z * JOWN + four - 1.0, -1.0)
        place[:, g * LANES : (g + 1) * LANES] = ones_where(iota((NZ * JOWN, LANES), 0) == key)

    sent = pl.ds(0, (ncomp - 1) * 16)
    flange_wait = pltpu.make_async_remote_copy(
        flange_send.at[sent], flange_recv.at[sent], flange_sem.at[0], flange_sem.at[1],
        **to(comp, other),
    )
    flange_wait.wait_recv()
    relay[...] = flange_recv[...].astype(f32)

    def rows_copy(k, e, jj, b):
        dest = lax.rem(plane + k, nplane)
        return pltpu.make_async_remote_copy(
            rows_send.at[e * quarter + jj, pl.ds(pl.multiple_of(dest * group, group), group)],
            rows_recv.at[jj, pl.ds(pl.multiple_of(here * group, group), group)],
            rows_send_sem, rows_recv_sem.at[jj], **to(dest * NZ + zpos, b),
        )

    for jj in range(quarter):
        for e in range(2):
            j = e * quarter + jj
            part = relay[pl.ds(j, fslots, stride=chunks), :].astype(bf16)
            span = slice(jj * LANES, (jj + 1) * LANES)
            incoming[e, :, span] = part
            rows_send[j] = (
                joint_base[e, :, span] - joint_bolt[...] * dot(joint_flange[...], part)
            ).astype(bf16)

            def send_rows(k, carry, e=e, jj=jj):
                rows_copy(k, e, jj, jnp.int32(e)).start()
                return carry

            lax.fori_loop(1, nplane, send_rows, 0)

            @pl.when(half != e)
            def _(e=e, jj=jj):
                rows_copy(0, e, jj, jnp.int32(e)).start()

            @pl.when(half == e)
            def _(jj=jj, j=j):
                rows_recv[jj, pl.ds(pl.multiple_of(here * group, group), group), :] = rows_send[
                    j, pl.ds(pl.multiple_of(plane * group, group), group), :
                ]

    step = 256

    def round_rows(which, m):
        at = pl.ds(pl.multiple_of(m * step, step), step)
        partner = dot(select_row[at, :], incoming[which])
        return (base[which, at, :] - bolt[at, 0:1] * partner).astype(bf16)

    def round_other(m, carry):
        round_send[pl.ds(pl.multiple_of(m * step, step), step), :] = round_rows(other, m)
        return carry

    def round_own(m, carry):
        at = pl.ds(pl.multiple_of(half * rows + m * step, step), step)
        round_full[at, :] = round_rows(half, m)
        return carry

    lax.fori_loop(0, rows // step, round_other, 0)
    round_copy = pltpu.make_async_remote_copy(
        round_send, round_full.at[own_rows], round_sem.at[0], round_sem.at[1], **to(comp, other)
    )
    round_copy.start()
    lax.fori_loop(0, rows // step, round_own, 0)

    factor = 1.0 / math.sqrt(2 * rows)
    got_rows = pl.ds(0, (2 * nplane - 1) * group)
    width = iface // quarter
    copies_out = []
    for jj in range(quarter):
        landed = rows_recv.at[jj, got_rows]
        pltpu.make_async_remote_copy(
            landed, landed, rows_send_sem, rows_recv_sem.at[jj], **to(comp, other)
        ).wait_recv()
        part_send[jj] = dot(place[...], rows_recv[jj]).astype(bf16)
        mine = pl.ds(pl.multiple_of(zpos * JOWN, JOWN), JOWN)
        part_recv[jj, mine, :] = part_send[jj, mine, :]

        def send_part(k, carry, jj=jj):
            dest = lax.rem(zpos + k, NZ)
            pltpu.make_async_remote_copy(
                part_send.at[jj, pl.ds(pl.multiple_of(dest * JOWN, JOWN), JOWN)],
                part_recv.at[jj, pl.ds(pl.multiple_of(zpos * JOWN, JOWN), JOWN)],
                part_send_sem, part_recv_sem.at[jj], **to(plane * NZ + dest, half),
            ).start()
            return carry

        lax.fori_loop(1, NZ, send_part, 0)
        if jj == 0:
            round_copy.wait()
        span = slice(jj * width, (jj + 1) * width)
        reduced[span, :] = (
            lax.dot_general(
                whole[:, :, span].reshape(2 * rows, width), round_full[...], (((0,), (0,)), ((), ())),
                preferred_element_type=f32,
            )
            * factor
        )
        copy_out = pltpu.make_async_copy(
            reduced.at[span], reduced_hbm.at[0, span], out_sem.at[jj]
        )
        copy_out.start()
        copies_out.append(copy_out)

    for jj in range(quarter):
        landed = part_recv.at[jj, pl.ds(0, (NZ - 1) * JOWN)]
        pltpu.make_async_remote_copy(
            landed, landed, part_send_sem, part_recv_sem.at[jj], **to(comp, other)
        ).wait_recv()
        total = part_recv[jj, 0:JOWN, :].astype(f32)
        for z in range(1, NZ):
            total = total + part_recv[jj, z * JOWN : (z + 1) * JOWN, :].astype(f32)
        forces[:, jj * LANES : (jj + 1) * LANES] = total

    flange_wait.wait_send()
    id_wait.wait_send()

    for jj in range(quarter):
        gone = rows_recv.at[jj, got_rows]
        pltpu.make_async_remote_copy(
            gone, gone, rows_send_sem, rows_recv_sem.at[jj], **to(comp, other)
        ).wait_send()
        gone = part_recv.at[jj, pl.ds(0, (NZ - 1) * JOWN)]
        pltpu.make_async_remote_copy(
            gone, gone, part_send_sem, part_recv_sem.at[jj], **to(comp, other)
        ).wait_send()
    for copy_out in copies_out:
        copy_out.wait()


def body(*args):
    modes, stiff = args[0], args[1]
    ncomp = lax.axis_size("comp")
    rows, iface = modes.shape[1:]
    cols = iface // 2
    quarter = cols // LANES
    width = stiff.shape[2]
    fslots, jslots = ncomp * FCAP, ncomp * JCAP
    nplane = ncomp // NZ
    dma = pltpu.SemaphoreType.DMA
    vmem = pl.BlockSpec(memory_space=pltpu.VMEM)
    hbm = pl.BlockSpec(memory_space=pl.ANY)
    scratch = [
        pltpu.VMEM((2 * rows // BLOCK, BLOCK, iface), bf16),
        pltpu.VMEM((rows, width), bf16),
        pltpu.VMEM((8, LANES), f32),
        pltpu.VMEM((ncomp * 16, LANES), bf16),
        pltpu.VMEM((ncomp * 16, LANES), bf16),
        pltpu.VMEM((ncomp * 16, LANES), f32),
        pltpu.VMEM((2, fslots, cols), bf16),
        pltpu.VMEM((2, rows, cols), f32),
        pltpu.VMEM((2, rows, cols), bf16),
        pltpu.VMEM((2, rows, cols), bf16),
        pltpu.VMEM((rows, LANES), f32),
        pltpu.VMEM((rows, fslots), bf16),
        pltpu.VMEM((jslots, rows), bf16),
        pltpu.VMEM((jslots, fslots), bf16),
        pltpu.VMEM((jslots, LANES), f32),
        pltpu.VMEM((2, jslots, cols), f32),
        pltpu.VMEM((nplane, 1, LANES), f32),
        pltpu.VMEM((2 * nplane, 1, LANES), f32),
        pltpu.VMEM((NZ * JOWN, 2 * nplane * NZ * JCAP), bf16),
        pltpu.VMEM((2 * quarter, jslots, LANES), bf16),
        pltpu.VMEM((quarter, 2 * jslots, LANES), bf16),
        pltpu.VMEM((rows, cols), bf16),
        pltpu.VMEM((2 * rows, cols), bf16),
        pltpu.VMEM((quarter, NZ * JOWN, LANES), bf16),
        pltpu.VMEM((quarter, NZ * JOWN, LANES), bf16),
        pltpu.VMEM((iface, cols), f32),
        dma((2,)), dma((2,)), dma((2,)), dma((2,)), dma, dma((quarter,)),
        dma((2,)), dma, dma((quarter,)), dma((quarter,)),
    ]
    return pl.pallas_call(
        kernel,
        out_shape=(
            jax.ShapeDtypeStruct((1, iface, cols), f32),
            jax.ShapeDtypeStruct((JOWN, cols), f32),
        ),
        in_specs=[hbm, hbm, pl.BlockSpec(memory_space=pltpu.SMEM)] + [vmem] * 7,
        out_specs=(hbm, vmem),
        scratch_shapes=scratch,
        compiler_params=pltpu.CompilerParams(
            collective_id=0, has_side_effects=True, vmem_limit_bytes=56 << 20
        ),
    )(modes.reshape(rows // BLOCK, BLOCK, iface), *args[1:])


def solution(mesh):
    placed = (
        P("comp", "blk", None),
        P("comp", "blk", None),
        P("comp", "blk", None),
        P("comp", "blk"),
        P("comp", "blk"),
        P("comp", "blk"),
        P("comp", "blk"),
        P("comp", "blk"),
        P("comp", "blk"),
        P("comp", "blk"),
    )
    return jax.shard_map(
        body,
        mesh=mesh,
        in_specs=placed,
        out_specs=(P("comp", None, "blk"), P("comp", "blk")),
        check_vma=False,
    )
```

profile of v0, /device:TPU:1, one launch (start us, length us, event | category | flops | bytes accessed | tf_op | source)
XLA Modules:
  0.0 60.0 jit_solution(16367319744667976438)
XLA Ops:
  0.6 1.4 %copy.12.block_cols = s32[1,16,8]{2,1,0:T(8,128)} copy(s32[1,16,8]{1,2,0:T(8,128)} %param.12) | data formatting | bytes 1024 | tf_op args[2]
  2.0 54.2 %shard_map.113 = (f32[1,1024,512]{2,1,0:T(8,128)}, f32[64,512]{1,0:T(8,128)}) custom-call(bf16[16,64,1024]{2,1,0:T(8,128)(2,1)} %bitcast.1, bf16[1,1024,512]{2,1,0:T(8,128)(2,1)} %stiff_hbm.1, s32[1,16,8]{2,1,0:T(8,128)} %copy.12.block_cols, s32[1,126]{1,0:T(1,128)} %flange_rows.1, s32[1,126]{1,0:T(1,128)} %flange_dest.1, s32[1,126]{1,0:T(1,128)} %flange_match.1, ...), custom_call_target="tpu_custom_call" | custom-call | tf_op jit(solution)/shard_map/pallas_call | solution.py:397
  56.2 0.0 copy-start
  56.2 3.1 %copy.15 = f32[1,1024,512]{2,1,0:T(8,128)} copy(f32[1,1024,512]{2,1,0:T(8,128)} %get-tuple-element.4) | data formatting | bytes 4194304
  59.3 0.0 copy-done
  59.3 0.7 %copy.16 = f32[64,512]{1,0:T(8,128)} copy(f32[64,512]{1,0:T(8,128)S(1)} %copy-done) | data formatting | bytes 262144
Async XLA Ops:
  56.2 3.1 %copy-start = (f32[64,512]{1,0:T(8,128)S(1)}, f32[64,512]{1,0:T(8,128)}, u32[]{:S(2)}) copy-start(f32[64,512]{1,0:T(8,128)} %get-tuple-element.5) | copy-start | bytes 393220
where the time goes:
time: 60.2 us; the launch traced here: 60 us
  Pallas kernels  54.2 us (90%)
  local copies, waits for them, and re-layouts  5.13 us (9%)
  between operations  0.65 us (1%)
    pallas_call x1, Pallas kernels, body(): pl.pallas_call(kernel, out_shape=(jax.ShapeDtypeStruct((1, iface, cols),...  54.2 us
    unnamed x5, local copies, waits for them, and re-layouts  5.13 us

commit v1 on v0

--- a/solution.py
+++ b/solution.py
@@ -39,13 +39,13 @@
 def kernel(
     modes_hbm, stiff_hbm, block_cols, flange_rows, flange_dest, flange_match, flange_stiff,
     joint_rows, joint_owner, joint_local,
-    reduced_hbm, forces,
-    whole, stiff, vec, flange_send, flange_recv, relay, incoming, base, high, low,
+    reduced, forces,
+    whole, stiff, vec, over_plane, plane_recv, regroup, over_z, z_recv, incoming, base, high, low,
     bolt, select_row, joint_select, joint_flange, joint_bolt, joint_base,
     id_send, id_recv, place, rows_send, rows_recv, round_send, round_full,
-    part_send, part_recv, reduced,
-    load_sem, flange_sem, modes_sem, id_sem, rows_send_sem, rows_recv_sem,
-    round_sem, part_send_sem, part_recv_sem, out_sem,
+    part_send, part_recv,
+    load_sem, plane_sem, plane_recv_sem, z_sem, z_recv_sem, modes_sem, id_sem, rows_send_sem, rows_recv_sem,
+    round_sem, part_send_sem, part_recv_sem,
 ):
     ncomp = lax.axis_size("comp")
     nplane = ncomp // NZ
@@ -76,22 +76,28 @@
 
     barrier = pltpu.get_barrier_semaphore()
 
-    def greet(k, carry):
-        pl.semaphore_signal(barrier, inc=1, **to(lax.rem(comp + k, ncomp), half))
+    def greet_z(k, carry):
+        pl.semaphore_signal(barrier, inc=1, **to(plane * NZ + lax.rem(zpos + k, NZ), half))
         return carry
 
     def greet_plane(k, carry):
-        pl.semaphore_signal(barrier, inc=1, **to(k * NZ + zpos, other))
-        return carry
-
-    lax.fori_loop(1, ncomp, greet, 0)
-    lax.fori_loop(0, nplane, greet_plane, 0)
+        there = lax.rem(plane + k, nplane) * NZ + zpos
+        pl.semaphore_signal(barrier, inc=1, **to(there, other))
+        pl.semaphore_signal(barrier, inc=1, **to(there, half))
+        return carry
+
+    lax.fori_loop(1, NZ, greet_z, 0)
+    lax.fori_loop(1, nplane, greet_plane, 0)
+    pl.semaphore_signal(barrier, inc=1, **to(comp, other))
 
     vec[...] = jnp.full(vec.shape, -1.0, f32)
     parity = lax.broadcasted_iota(jnp.int32, (1, nflange), 1) & 1
     vec[0:1, 0:nflange] = flange_rows[...].astype(f32)
     vec[1:2, 0:nflange] = (flange_dest[...] * FCAP + parity).astype(f32)
-    vec[2:3, 0:nflange] = (flange_dest[...] * FCAP + (flange_match[...] & 1)).astype(f32)
+    vec[2:3, 0:nflange] = (
+        ((flange_dest[...] & (NZ - 1)) * nplane + flange_dest[...] // NZ) * FCAP
+        + (flange_match[...] & 1)
+    ).astype(f32)
     vec[3:4, 0:nflange] = flange_stiff[...]
     frow, out_slot, in_slot, fstiff = vec[0:1, :], vec[1:2, :], vec[2:3, :], vec[3:4, :]
     row_of_slot = jnp.sum(
@@ -99,33 +105,72 @@
     ) - 1.0
     pick = ones_where(row_of_slot == iota((fslots, rows), 1))
     load_modes.wait()
+    pair = NZ * FCAP
+    line = nplane * FCAP
+    in_plane = pl.ds(pl.multiple_of(plane * pair, pair), pair)
+    in_line = pl.ds(pl.multiple_of(zpos * line, line), line)
+    order = [e * quarter + jj for jj in range(quarter) for e in range(2)]
+
+    def gather(j):
+        got = dot(pick, whole[own_blocks, :, j * LANES : (j + 2) * LANES].reshape(rows, 2 * LANES))
+        for i in range(2):
+            over_plane[j + i] = got[:, i * LANES : (i + 1) * LANES].astype(bf16)
+            plane_recv[j + i, in_plane, :] = over_plane[j + i, in_plane, :]
+
+    def send_over_plane(j):
+        def send(k, carry):
+            dest = lax.rem(plane + k, nplane)
+            pltpu.make_async_remote_copy(
+                over_plane.at[j, pl.ds(pl.multiple_of(dest * pair, pair), pair)],
+                plane_recv.at[j, in_plane],
+                plane_sem, plane_recv_sem.at[j], **to(dest * NZ + zpos, half),
+            ).start()
+            return carry
+
+        lax.fori_loop(1, nplane, send, 0)
+
     for j in range(0, chunks, 2):
-        got = dot(pick, whole[own_blocks, :, j * LANES : (j + 2) * LANES].reshape(rows, 2 * LANES))
-        relay[pl.ds(j, fslots, stride=chunks), :] = got[:, :LANES]
-        relay[pl.ds(j + 1, fslots, stride=chunks), :] = got[:, LANES:]
-    flange_send[...] = relay[...].astype(bf16)
-    flange_recv[pl.ds(pl.multiple_of(comp * 16, 16), 16), :] = jnp.zeros((16, LANES), bf16)
-
-    pl.semaphore_wait(barrier, ncomp - 1 + nplane)
-
-    def flange_copy(k):
-        dest = lax.rem(comp + k, ncomp)
-        return pltpu.make_async_remote_copy(
-            flange_send.at[pl.ds(pl.multiple_of(dest * 16, 16), 16)],
-            flange_recv.at[pl.ds(pl.multiple_of(comp * 16, 16), 16)],
-            flange_sem.at[0], flange_sem.at[1], **to(dest, half),
-        )
-
-    def send_flange(k, carry):
-        flange_copy(k).start()
-        return carry
-
-    lax.fori_loop(1, ncomp, send_flange, 0)
-
+        gather(j)
+
+    pl.semaphore_wait(barrier, NZ - 1 + 2 * nplane - 1)
     modes_copy = pltpu.make_async_remote_copy(
         whole.at[own_blocks], whole.at[own_blocks], modes_sem.at[0], modes_sem.at[1], **to(comp, other)
     )
     modes_copy.start()
+    for j in order:
+        send_over_plane(j)
+
+    turn = lax.broadcasted_iota(jnp.int32, (fslots, fslots), 0)
+    turned = ((turn // FCAP) & (nplane - 1)) * pair + turn // line * FCAP + (turn & (FCAP - 1))
+    regroup[...] = ones_where(turned == lax.broadcasted_iota(jnp.int32, (fslots, fslots), 1))
+
+    def plane_wait(j):
+        landed = plane_recv.at[j, pl.ds(0, (nplane - 1) * pair)]
+        return pltpu.make_async_remote_copy(
+            landed, landed, plane_sem, plane_recv_sem.at[j], **to(comp, other)
+        )
+
+    def z_wait(j):
+        landed = z_recv.at[j, pl.ds(0, (NZ - 1) * line)]
+        return pltpu.make_async_remote_copy(
+            landed, landed, z_sem, z_recv_sem.at[j], **to(comp, other)
+        )
+
+    def pass_on(j):
+        plane_wait(j).wait_recv()
+        over_z[j] = dot(regroup[...], plane_recv[j]).astype(bf16)
+        z_recv[j, in_line, :] = over_z[j, in_line, :]
+
+        def send(k, carry):
+            dest = lax.rem(zpos + k, NZ)
+            pltpu.make_async_remote_copy(
+                over_z.at[j, pl.ds(pl.multiple_of(dest * line, line), line)],
+                z_recv.at[j, in_line],
+                z_sem, z_recv_sem.at[j], **to(plane * NZ + dest, half),
+            ).start()
+            return carry
+
+        lax.fori_loop(1, NZ, send, 0)
 
     owner = joint_owner[...].astype(f32)
     local = joint_local[...].astype(f32)
@@ -162,6 +207,8 @@
 
     id_copy(0, other).start()
     lax.fori_loop(1, nplane, send_ids, 0)
+
+    pass_on(order[0])
 
     at_row = iota((rows, LANES), 0) == frow
     slot_of_row = jnp.sum(jnp.where(at_row, in_slot + 1.0, 0.0), axis=1, keepdims=True) - 1.0
@@ -184,6 +231,8 @@
         jnp.sum(jnp.where(takes, bolts_along, 0.0), axis=1, keepdims=True), joint_bolt.shape
     )
 
+    pass_on(order[1])
+
     load_stiff.wait()
     modes_copy.wait()
 
@@ -191,7 +240,7 @@
         at = pl.ds(pl.multiple_of(r * BLOCK, BLOCK), BLOCK)
         taken = jnp.concatenate(
             [
-                whole[block_cols[0, r, k]]
+                whole[block_cols[0, k, r]]
                 for k in range(NEIGH)
             ],
             axis=0,
@@ -207,9 +256,12 @@
             low[e, at, :] = rest[:, here_cols]
         return carry
 
-    lax.fori_loop(0, rows // BLOCK, block_row, 0)
-    for e in range(2):
-        joint_base[e] = dot(joint_select[...], high[e]) + dot(joint_select[...], low[e])
+    pieces = 3
+    at_piece = [p * nblocks // pieces for p in range(pieces + 1)]
+    for p in range(pieces):
+        lax.fori_loop(at_piece[p], at_piece[p + 1], block_row, 0)
+        pass_on(order[2 + 2 * p])
+        pass_on(order[3 + 2 * p])
 
     id_all = id_recv.at[pl.ds(0, 2 * nplane - 1)]
     id_wait = pltpu.make_async_remote_copy(
@@ -222,14 +274,6 @@
         key = jnp.where(four > 0.5, lane_z * JOWN + four - 1.0, -1.0)
         place[:, g * LANES : (g + 1) * LANES] = ones_where(iota((NZ * JOWN, LANES), 0) == key)
 
-    sent = pl.ds(0, (ncomp - 1) * 16)
-    flange_wait = pltpu.make_async_remote_copy(
-        flange_send.at[sent], flange_recv.at[sent], flange_sem.at[0], flange_sem.at[1],
-        **to(comp, other),
-    )
-    flange_wait.wait_recv()
-    relay[...] = flange_recv[...].astype(f32)
-
     def rows_copy(k, e, jj, b):
         dest = lax.rem(plane + k, nplane)
         return pltpu.make_async_remote_copy(
@@ -241,7 +285,13 @@
     for jj in range(quarter):
         for e in range(2):
             j = e * quarter + jj
-            part = relay[pl.ds(j, fslots, stride=chunks), :].astype(bf16)
+            if jj % 2 == 0:
+                two = slice(jj * LANES, (jj + 2) * LANES)
+                joint_base[e, :, two] = dot(joint_select[...], high[e, :, two]) + dot(
+                    joint_select[...], low[e, :, two]
+                )
+            z_wait(j).wait_recv()
+            part = z_recv[j]
             span = slice(jj * LANES, (jj + 1) * LANES)
             incoming[e, :, span] = part
             rows_send[j] = (
@@ -290,7 +340,6 @@
     factor = 1.0 / math.sqrt(2 * rows)
     got_rows = pl.ds(0, (2 * nplane - 1) * group)
     width = iface // quarter
-    copies_out = []
     for jj in range(quarter):
         landed = rows_recv.at[jj, got_rows]
         pltpu.make_async_remote_copy(
@@ -313,18 +362,13 @@
         if jj == 0:
             round_copy.wait()
         span = slice(jj * width, (jj + 1) * width)
-        reduced[span, :] = (
+        reduced[0, span, :] = (
             lax.dot_general(
                 whole[:, :, span].reshape(2 * rows, width), round_full[...], (((0,), (0,)), ((), ())),
                 preferred_element_type=f32,
             )
             * factor
         )
-        copy_out = pltpu.make_async_copy(
-            reduced.at[span], reduced_hbm.at[0, span], out_sem.at[jj]
-        )
-        copy_out.start()
-        copies_out.append(copy_out)
 
     for jj in range(quarter):
         landed = part_recv.at[jj, pl.ds(0, (NZ - 1) * JOWN)]
@@ -336,7 +380,9 @@
             total = total + part_recv[jj, z * JOWN : (z + 1) * JOWN, :].astype(f32)
         forces[:, jj * LANES : (jj + 1) * LANES] = total
 
-    flange_wait.wait_send()
+    for j in order:
+        plane_wait(j).wait_send()
+        z_wait(j).wait_send()
     id_wait.wait_send()
 
     for jj in range(quarter):
@@ -348,8 +394,6 @@
         pltpu.make_async_remote_copy(
             gone, gone, part_send_sem, part_recv_sem.at[jj], **to(comp, other)
         ).wait_send()
-    for copy_out in copies_out:
-        copy_out.wait()
 
 
 def body(*args):
@@ -358,6 +402,7 @@
     rows, iface = modes.shape[1:]
     cols = iface // 2
     quarter = cols // LANES
+    chunks = 2 * quarter
     width = stiff.shape[2]
     fslots, jslots = ncomp * FCAP, ncomp * JCAP
     nplane = ncomp // NZ
@@ -368,9 +413,11 @@
         pltpu.VMEM((2 * rows // BLOCK, BLOCK, iface), bf16),
         pltpu.VMEM((rows, width), bf16),
         pltpu.VMEM((8, LANES), f32),
-        pltpu.VMEM((ncomp * 16, LANES), bf16),
-        pltpu.VMEM((ncomp * 16, LANES), bf16),
-        pltpu.VMEM((ncomp * 16, LANES), f32),
+        pltpu.VMEM((chunks, fslots, LANES), bf16),
+        pltpu.VMEM((chunks, fslots, LANES), bf16),
+        pltpu.VMEM((fslots, fslots), bf16),
+        pltpu.VMEM((chunks, fslots, LANES), bf16),
+        pltpu.VMEM((chunks, fslots, LANES), bf16),
         pltpu.VMEM((2, fslots, cols), bf16),
         pltpu.VMEM((2, rows, cols), f32),
         pltpu.VMEM((2, rows, cols), bf16),
@@ -390,23 +437,23 @@
         pltpu.VMEM((2 * rows, cols), bf16),
         pltpu.VMEM((quarter, NZ * JOWN, LANES), bf16),
         pltpu.VMEM((quarter, NZ * JOWN, LANES), bf16),
-        pltpu.VMEM((iface, cols), f32),
-        dma((2,)), dma((2,)), dma((2,)), dma((2,)), dma, dma((quarter,)),
-        dma((2,)), dma, dma((quarter,)), dma((quarter,)),
+        dma((2,)), dma, dma((chunks,)), dma, dma((chunks,)),
+        dma((2,)), dma((2,)), dma, dma((quarter,)),
+        dma((2,)), dma, dma((quarter,)),
     ]
     return pl.pallas_call(
         kernel,
         out_shape=(
-            jax.ShapeDtypeStruct((1, iface, cols), f32),
-            jax.ShapeDtypeStruct((JOWN, cols), f32),
+            pltpu.VMEM((1, iface, cols), f32),
+            pltpu.VMEM((JOWN, cols), f32),
         ),
         in_specs=[hbm, hbm, pl.BlockSpec(memory_space=pltpu.SMEM)] + [vmem] * 7,
-        out_specs=(hbm, vmem),
+        out_specs=(vmem, vmem),
         scratch_shapes=scratch,
         compiler_params=pltpu.CompilerParams(
             collective_id=0, has_side_effects=True, vmem_limit_bytes=56 << 20
         ),
-    )(modes.reshape(rows // BLOCK, BLOCK, iface), *args[1:])
+    )(modes.reshape(rows // BLOCK, BLOCK, iface), stiff, jnp.swapaxes(args[2], 1, 2), *args[3:])
 
 
 def solution(mesh):

time: 60.2 us -> 54 us (0.90)
  local copies, waits for them, and re-layouts: 5.13 us -> 1.98 us
  Pallas kernels: 54.2 us -> 51.3 us
    unnamed x5 -> x2, local copies, waits for them, and re-layouts: 5.13 us -> 1.98 us
    pallas_call x1, Pallas kernels: 54.2 us -> 51.3 us  [body(): pl.pallas_call(kernel, out_shape=(pltpu.VMEM((1, iface, cols), f32), pltp...]
where the time goes in v1:
time: 54 us; the launch traced here: 53.9 us
  Pallas kernels  51.3 us (95%)
  local copies, waits for them, and re-layouts  1.98 us (4%)
  between operations  0.64 us (1%)
    pallas_call x1, Pallas kernels, body(): pl.pallas_call(kernel, out_shape=(pltpu.VMEM((1, iface, cols), f32), pltp...  51.3 us
    unnamed x2, local copies, waits for them, and re-layouts  1.98 us

profile of v1, /device:TPU:1, one launch (start us, length us, event | category | flops | bytes accessed | tf_op | source)
XLA Modules:
  0.0 53.9 jit_solution(13018524695151199266)
XLA Ops:
  0.6 51.3 %shard_map.113 = (f32[1,1024,512]{2,1,0:T(8,128)S(1)}, f32[64,512]{1,0:T(8,128)S(1)}) custom-call(bf16[16,64,1024]{2,1,0:T(8,128)(2,1)} %bitcast.2, bf16[1,1024,512]{2,1,0:T(8,128)(2,1)} %stiff_hbm.1, s32[1,8,16]{2,1,0:T(8,128)} %bitcast.3, s32[1,126]{1,0:T(1,128)} %flange_rows.1, s32[1,126]{1,0:T(1,128)} %flange_dest.1, s32[1,126]{1,0:T(1,128)} %flange_match.1, ...), custom_call_target="tpu_custom_call" | custom-call | tf_op jit(solution)/shard_map/pallas_call | solution.py:444
  51.9 1.3 %copy.14 = f32[1,1024,512]{2,1,0:T(8,128)} copy(f32[1,1024,512]{2,1,0:T(8,128)S(1)} %get-tuple-element.2) | data formatting | bytes 4194304
  53.2 0.7 %copy.15 = f32[64,512]{1,0:T(8,128)} copy(f32[64,512]{1,0:T(8,128)S(1)} %get-tuple-element.3) | data formatting | bytes 262144

commit v2 on v1

--- a/solution.py
+++ b/solution.py
@@ -37,14 +37,16 @@
 
 
 def kernel(
-    modes_hbm, stiff_hbm, block_cols, flange_rows, flange_dest, flange_match, flange_stiff,
+    modes_hbm, stiff_hbm, block_cols_hbm, flange_rows_hbm, flange_dest_hbm, flange_match_hbm,
+    flange_stiff_hbm, joint_rows_hbm, joint_owner_hbm, joint_local_hbm,
+    reduced, forces,
+    block_cols, flange_rows, flange_dest, flange_match, flange_stiff,
     joint_rows, joint_owner, joint_local,
-    reduced, forces,
     whole, stiff, vec, over_plane, plane_recv, regroup, over_z, z_recv, incoming, base, high, low,
     bolt, select_row, joint_select, joint_flange, joint_bolt, joint_base,
     id_send, id_recv, place, rows_send, rows_recv, round_send, round_full,
     part_send, part_recv,
-    load_sem, plane_sem, plane_recv_sem, z_sem, z_recv_sem, modes_sem, id_sem, rows_send_sem, rows_recv_sem,
+    load_sem, small_sem, plane_sem, plane_recv_sem, z_sem, z_recv_sem, modes_sem, id_sem, rows_send_sem, rows_recv_sem,
     round_sem, part_send_sem, part_recv_sem,
 ):
     ncomp = lax.axis_size("comp")
@@ -71,7 +73,26 @@
 
     load_modes = pltpu.make_async_copy(modes_hbm, whole.at[own_blocks], load_sem.at[0])
     load_stiff = pltpu.make_async_copy(stiff_hbm.at[0], stiff, load_sem.at[1])
+    loads = [
+        pltpu.make_async_copy(source, target, small_sem.at[i])
+        for i, (source, target) in enumerate(
+            (
+                (flange_rows_hbm, flange_rows),
+                (flange_dest_hbm, flange_dest),
+                (flange_match_hbm, flange_match),
+                (flange_stiff_hbm, flange_stiff),
+                (joint_rows_hbm, joint_rows),
+                (joint_owner_hbm, joint_owner),
+                (joint_local_hbm, joint_local),
+                (block_cols_hbm, block_cols),
+            )
+        )
+    ]
+    for load in loads[:4]:
+        load.start()
     load_modes.start()
+    for load in loads[4:]:
+        load.start()
     load_stiff.start()
 
     barrier = pltpu.get_barrier_semaphore()
@@ -86,10 +107,12 @@
         pl.semaphore_signal(barrier, inc=1, **to(there, half))
         return carry
 
-    lax.fori_loop(1, NZ, greet_z, 0)
-    lax.fori_loop(1, nplane, greet_plane, 0)
+    lax.fori_loop(1, NZ, greet_z, 0, unroll=7)
+    lax.fori_loop(1, nplane, greet_plane, 0, unroll=5)
     pl.semaphore_signal(barrier, inc=1, **to(comp, other))
 
+    for load in loads[:4]:
+        load.wait()
     vec[...] = jnp.full(vec.shape, -1.0, f32)
     parity = lax.broadcasted_iota(jnp.int32, (1, nflange), 1) & 1
     vec[0:1, 0:nflange] = flange_rows[...].astype(f32)
@@ -127,17 +150,21 @@
             ).start()
             return carry
 
-        lax.fori_loop(1, nplane, send, 0)
-
-    for j in range(0, chunks, 2):
-        gather(j)
+        lax.fori_loop(1, nplane, send, 0, unroll=5)
+
+    gather(0)
+    gather(quarter)
 
     pl.semaphore_wait(barrier, NZ - 1 + 2 * nplane - 1)
     modes_copy = pltpu.make_async_remote_copy(
         whole.at[own_blocks], whole.at[own_blocks], modes_sem.at[0], modes_sem.at[1], **to(comp, other)
     )
     modes_copy.start()
-    for j in order:
+    for j in order[:4]:
+        send_over_plane(j)
+    gather(2)
+    gather(quarter + 2)
+    for j in order[4:]:
         send_over_plane(j)
 
     turn = lax.broadcasted_iota(jnp.int32, (fslots, fslots), 0)
@@ -170,33 +197,38 @@
             ).start()
             return carry
 
-        lax.fori_loop(1, NZ, send, 0)
-
+        lax.fori_loop(1, NZ, send, 0, unroll=7)
+
+    for load in loads[4:7]:
+        load.wait()
     owner = joint_owner[...].astype(f32)
     local = joint_local[...].astype(f32)
     njoint = owner.shape[1]
     square = (njoint, njoint)
     before = (as_column(owner) == owner) & (iota(square, 0) < iota(square, 1))
     position = jnp.sum(jnp.where(before, 1.0, 0.0), axis=0, keepdims=True)
-    jslot = owner * JCAP + position
     group = NZ * JCAP
-    jslot_int = jslot.astype(jnp.int32)
-    lane = (jslot_int & (group - 1)) + (plane & 3) * group
+    unit = group // 2
+    owner_z = joint_owner[...] & (NZ - 1)
+    owner_plane = joint_owner[...] // NZ
+    slot_in_unit = (owner_z // 2) * JCAP + position.astype(jnp.int32)
+    jslot = (owner_plane * group + (owner_z & 1) * unit + slot_in_unit).astype(f32)
+    lane = slot_in_unit + (plane & 7) * unit
     of_plane = ones_where(
-        lax.broadcasted_iota(jnp.int32, (nplane, njoint), 0) == (joint_owner[...] // NZ)
+        lax.broadcasted_iota(jnp.int32, (2 * nplane, njoint), 0) == owner_plane * 2 + (owner_z & 1)
     )
     at_lane = jnp.where(
         lax.broadcasted_iota(jnp.int32, (LANES, njoint), 0) == lane, local + 1.0, 0.0
     ).astype(bf16)
     ids = lax.dot_general(of_plane, at_lane, (((1,), (1,)), ((), ())), preferred_element_type=f32)
-    for d in range(nplane):
+    for d in range(2 * nplane):
         id_send[d] = ids[d : d + 1, :]
-    id_recv[pl.ds(here, 1)] = id_send[pl.ds(plane, 1)]
+    id_recv[pl.ds(2 * here, 2)] = id_send[pl.ds(2 * plane, 2)]
 
     def id_copy(k, b):
         dest = lax.rem(plane + k, nplane)
         return pltpu.make_async_remote_copy(
-            id_send.at[pl.ds(dest, 1)], id_recv.at[pl.ds(here, 1)],
+            id_send.at[pl.ds(2 * dest, 2)], id_recv.at[pl.ds(2 * here, 2)],
             id_sem.at[0], id_sem.at[1], **to(dest * NZ + zpos, b),
         )
 
@@ -206,7 +238,7 @@
         return carry
 
     id_copy(0, other).start()
-    lax.fori_loop(1, nplane, send_ids, 0)
+    lax.fori_loop(1, nplane, send_ids, 0, unroll=5)
 
     pass_on(order[0])
 
@@ -232,87 +264,110 @@
     )
 
     pass_on(order[1])
-
+    pass_on(order[2])
+
+    loads[7].wait()
     load_stiff.wait()
     modes_copy.wait()
 
-    def block_row(r, carry):
-        at = pl.ds(pl.multiple_of(r * BLOCK, BLOCK), BLOCK)
-        taken = jnp.concatenate(
-            [
-                whole[block_cols[0, k, r]]
-                for k in range(NEIGH)
-            ],
-            axis=0,
-        )
-        own = whole[half * nblocks + r].astype(f32)
-        value = dot(stiff[at, :], taken) + bolt[at, 0:1] * own
-        top = value.astype(bf16)
-        rest = (value - top.astype(f32)).astype(bf16)
+    half_cols = cols // 2
+
+    def block_row(p):
+        def run(r, carry):
+            at = pl.ds(pl.multiple_of(r * BLOCK, BLOCK), BLOCK)
+            for e in range(2):
+                span = slice(e * cols + p * half_cols, e * cols + (p + 1) * half_cols)
+                two = slice(p * half_cols, (p + 1) * half_cols)
+                taken = jnp.concatenate(
+                    [whole[block_cols[0, k, r], :, span] for k in range(NEIGH)], axis=0
+                )
+                own = whole[half * nblocks + r, :, span].astype(f32)
+                value = dot(stiff[at, :], taken) + bolt[at, 0:1] * own
+                top = value.astype(bf16)
+                base[e, at, two] = value
+                high[e, at, two] = top
+                low[e, at, two] = (value - top.astype(f32)).astype(bf16)
+            return carry
+
+        return run
+
+    def base_rows(p):
+        two = slice(p * half_cols, (p + 1) * half_cols)
         for e in range(2):
-            here_cols = slice(e * cols, (e + 1) * cols)
-            base[e, at, :] = value[:, here_cols]
-            high[e, at, :] = top[:, here_cols]
-            low[e, at, :] = rest[:, here_cols]
-        return carry
-
-    pieces = 3
-    at_piece = [p * nblocks // pieces for p in range(pieces + 1)]
-    for p in range(pieces):
-        lax.fori_loop(at_piece[p], at_piece[p + 1], block_row, 0)
-        pass_on(order[2 + 2 * p])
-        pass_on(order[3 + 2 * p])
-
-    id_all = id_recv.at[pl.ds(0, 2 * nplane - 1)]
-    id_wait = pltpu.make_async_remote_copy(
-        id_all, id_all, id_sem.at[0], id_sem.at[1], **to(comp, other)
-    )
-    id_wait.wait_recv()
-    lane_z = ((lax.broadcasted_iota(jnp.int32, (1, LANES), 1) & (group - 1)) // JCAP).astype(f32)
-    for g in range(2 * nplane // 4):
-        four = id_recv[4 * g] + id_recv[4 * g + 1] + id_recv[4 * g + 2] + id_recv[4 * g + 3]
-        key = jnp.where(four > 0.5, lane_z * JOWN + four - 1.0, -1.0)
-        place[:, g * LANES : (g + 1) * LANES] = ones_where(iota((NZ * JOWN, LANES), 0) == key)
-
-    def rows_copy(k, e, jj, b):
+            joint_base[e, :, two] = dot(joint_select[...], high[e, :, two]) + dot(
+                joint_select[...], low[e, :, two]
+            )
+
+    def rows_copy(k, e, jj, g):
         dest = lax.rem(plane + k, nplane)
         return pltpu.make_async_remote_copy(
-            rows_send.at[e * quarter + jj, pl.ds(pl.multiple_of(dest * group, group), group)],
-            rows_recv.at[jj, pl.ds(pl.multiple_of(here * group, group), group)],
-            rows_send_sem, rows_recv_sem.at[jj], **to(dest * NZ + zpos, b),
+            rows_send.at[e * quarter + jj, pl.ds(pl.multiple_of(dest * group + g * unit, unit), unit)],
+            rows_recv.at[jj, g, pl.ds(pl.multiple_of(here * unit, unit), unit)],
+            rows_send_sem, rows_recv_sem.at[2 * jj + g], **to(dest * NZ + zpos, jnp.int32(e)),
         )
 
-    for jj in range(quarter):
+    def send_rows(e, jj, g):
+        def send(k, carry):
+            rows_copy(k, e, jj, g).start()
+            return carry
+
+        lax.fori_loop(1, nplane, send, 0, unroll=5)
+
+        @pl.when(half != e)
+        def _():
+            rows_copy(0, e, jj, g).start()
+
+        @pl.when(half == e)
+        def _():
+            rows_recv[jj, g, pl.ds(pl.multiple_of(here * unit, unit), unit), :] = rows_send[
+                e * quarter + jj, pl.ds(pl.multiple_of(plane * group + g * unit, unit), unit), :
+            ]
+
+    def joint_rows_out(jj):
+        span = slice(jj * LANES, (jj + 1) * LANES)
         for e in range(2):
             j = e * quarter + jj
-            if jj % 2 == 0:
-                two = slice(jj * LANES, (jj + 2) * LANES)
-                joint_base[e, :, two] = dot(joint_select[...], high[e, :, two]) + dot(
-                    joint_select[...], low[e, :, two]
-                )
             z_wait(j).wait_recv()
             part = z_recv[j]
-            span = slice(jj * LANES, (jj + 1) * LANES)
             incoming[e, :, span] = part
             rows_send[j] = (
                 joint_base[e, :, span] - joint_bolt[...] * dot(joint_flange[...], part)
             ).astype(bf16)
-
-            def send_rows(k, carry, e=e, jj=jj):
-                rows_copy(k, e, jj, jnp.int32(e)).start()
-                return carry
-
-            lax.fori_loop(1, nplane, send_rows, 0)
-
-            @pl.when(half != e)
-            def _(e=e, jj=jj):
-                rows_copy(0, e, jj, jnp.int32(e)).start()
-
-            @pl.when(half == e)
-            def _(jj=jj, j=j):
-                rows_recv[jj, pl.ds(pl.multiple_of(here * group, group), group), :] = rows_send[
-                    j, pl.ds(pl.multiple_of(plane * group, group), group), :
-                ]
+            send_rows(e, jj, 0)
+        for e in range(2):
+            send_rows(e, jj, 1)
+
+    lax.fori_loop(0, nblocks // 2, block_row(0), 0)
+    pass_on(order[3])
+    lax.fori_loop(nblocks // 2, nblocks, block_row(0), 0)
+    pass_on(order[4])
+    pass_on(order[5])
+    base_rows(0)
+    joint_rows_out(0)
+    pass_on(order[6])
+    pass_on(order[7])
+    joint_rows_out(1)
+    lax.fori_loop(0, nblocks, block_row(1), 0)
+    base_rows(1)
+    joint_rows_out(2)
+    joint_rows_out(3)
+
+    id_all = id_recv.at[pl.ds(0, 2 * (2 * nplane - 1))]
+    id_wait = pltpu.make_async_remote_copy(
+        id_all, id_all, id_sem.at[0], id_sem.at[1], **to(comp, other)
+    )
+    id_wait.wait_recv()
+    lane_z = ((lax.broadcasted_iota(jnp.int32, (1, LANES), 1) & (unit - 1)) // JCAP).astype(f32)
+    sources = LANES // unit
+    for g in range(2):
+        for b in range(2 * nplane // sources):
+            one = id_recv[2 * sources * b + g]
+            for i in range(1, sources):
+                one = one + id_recv[2 * (sources * b + i) + g]
+            key = jnp.where(one > 0.5, lane_z * JOWN + one - 1.0, -1.0)
+            place[g, :, b * LANES : (b + 1) * LANES] = ones_where(
+                iota((NZ // 2 * JOWN, LANES), 0) == key
+            )
 
     step = 256
 
@@ -335,33 +390,36 @@
         round_send, round_full.at[own_rows], round_sem.at[0], round_sem.at[1], **to(comp, other)
     )
     round_copy.start()
-    lax.fori_loop(0, rows // step, round_own, 0)
 
     factor = 1.0 / math.sqrt(2 * rows)
-    got_rows = pl.ds(0, (2 * nplane - 1) * group)
+    got_rows = pl.ds(0, (2 * nplane - 1) * unit)
     width = iface // quarter
-    for jj in range(quarter):
-        landed = rows_recv.at[jj, got_rows]
+
+    def add_up(jj, g):
+        landed = rows_recv.at[jj, g, got_rows]
         pltpu.make_async_remote_copy(
-            landed, landed, rows_send_sem, rows_recv_sem.at[jj], **to(comp, other)
+            landed, landed, rows_send_sem, rows_recv_sem.at[2 * jj + g], **to(comp, other)
         ).wait_recv()
-        part_send[jj] = dot(place[...], rows_recv[jj]).astype(bf16)
+        part_send[jj, g] = dot(place[g], rows_recv[jj, g]).astype(bf16)
         mine = pl.ds(pl.multiple_of(zpos * JOWN, JOWN), JOWN)
-        part_recv[jj, mine, :] = part_send[jj, mine, :]
-
-        def send_part(k, carry, jj=jj):
-            dest = lax.rem(zpos + k, NZ)
-            pltpu.make_async_remote_copy(
-                part_send.at[jj, pl.ds(pl.multiple_of(dest * JOWN, JOWN), JOWN)],
-                part_recv.at[jj, pl.ds(pl.multiple_of(zpos * JOWN, JOWN), JOWN)],
-                part_send_sem, part_recv_sem.at[jj], **to(plane * NZ + dest, half),
-            ).start()
-            return carry
-
-        lax.fori_loop(1, NZ, send_part, 0)
-        if jj == 0:
-            round_copy.wait()
-        span = slice(jj * width, (jj + 1) * width)
+        for q in range(NZ // 2):
+            dest = 2 * q + g
+            rows_there = pl.ds(q * JOWN, JOWN)
+
+            @pl.when(dest != zpos)
+            def _():
+                pltpu.make_async_remote_copy(
+                    part_send.at[jj, g, rows_there],
+                    part_recv.at[jj, mine],
+                    part_send_sem, part_recv_sem.at[jj], **to(plane * NZ + dest, half),
+                ).start()
+
+            @pl.when(dest == zpos)
+            def _():
+                part_recv[jj, mine, :] = part_send[jj, g, rows_there, :]
+
+    def project(piece):
+        span = slice(piece * width, (piece + 1) * width)
         reduced[0, span, :] = (
             lax.dot_general(
                 whole[:, :, span].reshape(2 * rows, width), round_full[...], (((0,), (0,)), ((), ())),
@@ -369,6 +427,21 @@
             )
             * factor
         )
+
+    add_up(0, 0)
+    add_up(0, 1)
+    lax.fori_loop(0, rows // step, round_own, 0)
+    add_up(1, 0)
+    add_up(1, 1)
+    round_copy.wait()
+    project(0)
+    project(1)
+    add_up(2, 0)
+    add_up(2, 1)
+    project(2)
+    add_up(3, 0)
+    add_up(3, 1)
+    project(3)
 
     for jj in range(quarter):
         landed = part_recv.at[jj, pl.ds(0, (NZ - 1) * JOWN)]
@@ -386,10 +459,11 @@
     id_wait.wait_send()
 
     for jj in range(quarter):
-        gone = rows_recv.at[jj, got_rows]
-        pltpu.make_async_remote_copy(
-            gone, gone, rows_send_sem, rows_recv_sem.at[jj], **to(comp, other)
-        ).wait_send()
+        for g in range(2):
+            gone = rows_recv.at[jj, g, got_rows]
+            pltpu.make_async_remote_copy(
+                gone, gone, rows_send_sem, rows_recv_sem.at[2 * jj + g], **to(comp, other)
+            ).wait_send()
         gone = part_recv.at[jj, pl.ds(0, (NZ - 1) * JOWN)]
         pltpu.make_async_remote_copy(
             gone, gone, part_send_sem, part_recv_sem.at[jj], **to(comp, other)
@@ -409,7 +483,9 @@
     dma = pltpu.SemaphoreType.DMA
     vmem = pl.BlockSpec(memory_space=pltpu.VMEM)
     hbm = pl.BlockSpec(memory_space=pl.ANY)
-    scratch = [
+    scratch = [pltpu.SMEM((1, NEIGH, rows // BLOCK), jnp.int32)]
+    scratch += [pltpu.VMEM(a.shape, a.dtype) for a in args[3:]]
+    scratch += [
         pltpu.VMEM((2 * rows // BLOCK, BLOCK, iface), bf16),
         pltpu.VMEM((rows, width), bf16),
         pltpu.VMEM((8, LANES), f32),
@@ -428,17 +504,17 @@
         pltpu.VMEM((jslots, fslots), bf16),
         pltpu.VMEM((jslots, LANES), f32),
         pltpu.VMEM((2, jslots, cols), f32),
-        pltpu.VMEM((nplane, 1, LANES), f32),
         pltpu.VMEM((2 * nplane, 1, LANES), f32),
-        pltpu.VMEM((NZ * JOWN, 2 * nplane * NZ * JCAP), bf16),
+        pltpu.VMEM((4 * nplane, 1, LANES), f32),
+        pltpu.VMEM((2, NZ // 2 * JOWN, jslots), bf16),
         pltpu.VMEM((2 * quarter, jslots, LANES), bf16),
-        pltpu.VMEM((quarter, 2 * jslots, LANES), bf16),
+        pltpu.VMEM((quarter, 2, jslots, LANES), bf16),
         pltpu.VMEM((rows, cols), bf16),
         pltpu.VMEM((2 * rows, cols), bf16),
+        pltpu.VMEM((quarter, 2, NZ // 2 * JOWN, LANES), bf16),
         pltpu.VMEM((quarter, NZ * JOWN, LANES), bf16),
-        pltpu.VMEM((quarter, NZ * JOWN, LANES), bf16),
-        dma((2,)), dma, dma((chunks,)), dma, dma((chunks,)),
-        dma((2,)), dma((2,)), dma, dma((quarter,)),
+        dma((2,)), dma((8,)), dma, dma((chunks,)), dma, dma((chunks,)),
+        dma((2,)), dma((2,)), dma, dma((chunks,)),
         dma((2,)), dma, dma((quarter,)),
     ]
     return pl.pallas_call(
@@ -447,7 +523,7 @@
             pltpu.VMEM((1, iface, cols), f32),
             pltpu.VMEM((JOWN, cols), f32),
         ),
-        in_specs=[hbm, hbm, pl.BlockSpec(memory_space=pltpu.SMEM)] + [vmem] * 7,
+        in_specs=[hbm] * 10,
         out_specs=(vmem, vmem),
         scratch_shapes=scratch,
         compiler_params=pltpu.CompilerParams(

time: 54 us -> 48.9 us (0.906)
  Pallas kernels: 51.3 us -> 46.2 us
    pallas_call x1, Pallas kernels: 51.3 us -> 46.2 us  [body(): pl.pallas_call(kernel, out_shape=(pltpu.VMEM((1, iface, cols), f32), pltp...]
where the time goes in v2:
time: 48.9 us
  Pallas kernels  46.2 us (94%)
  local copies, waits for them, and re-layouts  1.98 us (4%)
  between operations  0.64 us (1%)
    pallas_call x1, Pallas kernels, body(): pl.pallas_call(kernel, out_shape=(pltpu.VMEM((1, iface, cols), f32), pltp...  46.2 us
    unnamed x2, local copies, waits for them, and re-layouts  1.98 us

profile of v2, /device:TPU:1, one launch (start us, length us, event | category | flops | bytes accessed | tf_op | source)
XLA Modules:
  0.0 48.9 jit_solution(3589285976986608761)
XLA Ops:
  0.6 46.2 %shard_map.113 = (f32[1,1024,512]{2,1,0:T(8,128)S(1)}, f32[64,512]{1,0:T(8,128)S(1)}) custom-call(bf16[16,64,1024]{2,1,0:T(8,128)(2,1)} %bitcast.2, bf16[1,1024,512]{2,1,0:T(8,128)(2,1)} %stiff_hbm.1, s32[1,8,16]{2,1,0:T(8,128)} %bitcast.3, s32[1,126]{1,0:T(1,128)} %flange_rows_hbm.1, s32[1,126]{1,0:T(1,128)} %flange_dest_hbm.1, s32[1,126]{1,0:T(1,128)} %flange_match_hbm.1, ...), custom_call_target="tpu_custom_call" | custom-call | tf_op jit(solution)/shard_map/pallas_call | solution.py:520
  46.9 1.3 %copy.14 = f32[1,1024,512]{2,1,0:T(8,128)} copy(f32[1,1024,512]{2,1,0:T(8,128)S(1)} %get-tuple-element.2) | data formatting | bytes 4194304
  48.2 0.7 %copy.15 = f32[64,512]{1,0:T(8,128)} copy(f32[64,512]{1,0:T(8,128)S(1)} %get-tuple-element.3) | data formatting | bytes 262144

commit v3 on v2

--- a/solution.py
+++ b/solution.py
@@ -42,8 +42,8 @@
     reduced, forces,
     block_cols, flange_rows, flange_dest, flange_match, flange_stiff,
     joint_rows, joint_owner, joint_local,
-    whole, stiff, vec, over_plane, plane_recv, regroup, over_z, z_recv, incoming, base, high, low,
-    bolt, select_row, joint_select, joint_flange, joint_bolt, joint_base,
+    whole_0, whole_1, whole_2, whole_3, stiff, vec, over_plane, plane_recv, regroup, ungroup, over_z, z_recv, incoming, base, high, low,
+    bolt, select_row, joint_select, joint_flange, joint_bolt, joint_place, joint_base,
     id_send, id_recv, place, rows_send, rows_recv, round_send, round_full,
     part_send, part_recv,
     load_sem, small_sem, plane_sem, plane_recv_sem, z_sem, z_recv_sem, modes_sem, id_sem, rows_send_sem, rows_recv_sem,
@@ -56,8 +56,9 @@
     other = 1 - half
     plane = comp // NZ
     zpos = lax.rem(comp, NZ)
-    rows, iface = stiff.shape[0], whole.shape[2]
-    cols = iface // 2
+    whole = (whole_0, whole_1, whole_2, whole_3)
+    rows, cols = stiff.shape[0], forces.shape[1]
+    iface = 2 * cols
     nflange = flange_rows.shape[1]
     fslots = ncomp * FCAP
     jslots = ncomp * JCAP
@@ -71,8 +72,18 @@
     def to(c, b):
         return dict(device_id={"comp": c, "blk": b}, device_id_type=MESH)
 
-    load_modes = pltpu.make_async_copy(modes_hbm, whole.at[own_blocks], load_sem.at[0])
-    load_stiff = pltpu.make_async_copy(stiff_hbm.at[0], stiff, load_sem.at[1])
+    load_modes = [
+        [
+            pltpu.make_async_copy(
+                modes_hbm.at[:, :, pl.ds(e * cols + q * LANES, LANES)],
+                whole[q].at[own_blocks, :, pl.ds(e * LANES, LANES)],
+                load_sem.at[2 * q + e],
+            )
+            for e in range(2)
+        ]
+        for q in range(quarter)
+    ]
+    load_stiff = pltpu.make_async_copy(stiff_hbm.at[0], stiff, load_sem.at[chunks])
     loads = [
         pltpu.make_async_copy(source, target, small_sem.at[i])
         for i, (source, target) in enumerate(
@@ -90,7 +101,9 @@
     ]
     for load in loads[:4]:
         load.start()
-    load_modes.start()
+    for q in range(quarter):
+        for load in load_modes[q]:
+            load.start()
     for load in loads[4:]:
         load.start()
     load_stiff.start()
@@ -127,18 +140,27 @@
         jnp.where(iota((fslots, LANES), 0) == out_slot, frow + 1.0, 0.0), axis=1, keepdims=True
     ) - 1.0
     pick = ones_where(row_of_slot == iota((fslots, rows), 1))
-    load_modes.wait()
+    last = quarter - 1
     pair = NZ * FCAP
     line = nplane * FCAP
     in_plane = pl.ds(pl.multiple_of(plane * pair, pair), pair)
     in_line = pl.ds(pl.multiple_of(zpos * line, line), line)
-    order = [e * quarter + jj for jj in range(quarter) for e in range(2)]
-
-    def gather(j):
-        got = dot(pick, whole[own_blocks, :, j * LANES : (j + 2) * LANES].reshape(rows, 2 * LANES))
-        for i in range(2):
-            over_plane[j + i] = got[:, i * LANES : (i + 1) * LANES].astype(bf16)
-            plane_recv[j + i, in_plane, :] = over_plane[j + i, in_plane, :]
+
+    turn = lax.broadcasted_iota(jnp.int32, (fslots, fslots), 0)
+    turned = ((turn // FCAP) & (nplane - 1)) * pair + turn // line * FCAP + (turn & (FCAP - 1))
+    regroup[...] = ones_where(turned == lax.broadcasted_iota(jnp.int32, (fslots, fslots), 1))
+    back = ((turn // FCAP) & (NZ - 1)) * line + turn // pair * FCAP + (turn & (FCAP - 1))
+    ungroup[...] = ones_where(back == lax.broadcasted_iota(jnp.int32, (fslots, fslots), 1))
+
+    def gather(q):
+        for load in load_modes[q]:
+            load.wait()
+        got = dot(pick, whole[q][own_blocks].reshape(rows, 2 * LANES))
+        for e in range(2):
+            j = e * quarter + q
+            over_plane[j] = got[:, e * LANES : (e + 1) * LANES].astype(bf16)
+            if q < last:
+                plane_recv[j, in_plane, :] = over_plane[j, in_plane, :]
 
     def send_over_plane(j):
         def send(k, carry):
@@ -153,23 +175,30 @@
         lax.fori_loop(1, nplane, send, 0, unroll=5)
 
     gather(0)
-    gather(quarter)
 
     pl.semaphore_wait(barrier, NZ - 1 + 2 * nplane - 1)
-    modes_copy = pltpu.make_async_remote_copy(
-        whole.at[own_blocks], whole.at[own_blocks], modes_sem.at[0], modes_sem.at[1], **to(comp, other)
-    )
-    modes_copy.start()
-    for j in order[:4]:
-        send_over_plane(j)
-    gather(2)
-    gather(quarter + 2)
-    for j in order[4:]:
-        send_over_plane(j)
-
-    turn = lax.broadcasted_iota(jnp.int32, (fslots, fslots), 0)
-    turned = ((turn // FCAP) & (nplane - 1)) * pair + turn // line * FCAP + (turn & (FCAP - 1))
-    regroup[...] = ones_where(turned == lax.broadcasted_iota(jnp.int32, (fslots, fslots), 1))
+    modes_copies = [
+        pltpu.make_async_remote_copy(
+            whole[q].at[own_blocks], whole[q].at[own_blocks], modes_sem.at[0, q], modes_sem.at[1, q],
+            **to(comp, other),
+        )
+        for q in range(quarter)
+    ]
+    def send_all():
+        for e in range(2):
+            send_over_plane(e * quarter)
+        gather(last)
+        for e in range(2):
+            j = e * quarter + last
+            over_z[j] = dot(regroup[...], over_plane[j]).astype(bf16)
+            send_over_z(j)
+        modes_copies[0].start()
+        for q in range(1, last):
+            gather(q)
+            for e in range(2):
+                send_over_plane(e * quarter + q)
+            modes_copies[q].start()
+        modes_copies[last].start()
 
     def plane_wait(j):
         landed = plane_recv.at[j, pl.ds(0, (nplane - 1) * pair)]
@@ -183,9 +212,11 @@
             landed, landed, z_sem, z_recv_sem.at[j], **to(comp, other)
         )
 
-    def pass_on(j):
-        plane_wait(j).wait_recv()
-        over_z[j] = dot(regroup[...], plane_recv[j]).astype(bf16)
+    def pass_on(q):
+        for e in range(2):
+            pass_chunk(e * quarter + q)
+
+    def send_over_z(j):
         z_recv[j, in_line, :] = over_z[j, in_line, :]
 
         def send(k, carry):
@@ -198,6 +229,21 @@
             return carry
 
         lax.fori_loop(1, NZ, send, 0, unroll=7)
+
+    def pass_chunk(j):
+        if j % quarter < last:
+            plane_wait(j).wait_recv()
+            over_z[j] = dot(regroup[...], plane_recv[j]).astype(bf16)
+            send_over_z(j)
+        else:
+            z_wait(j).wait_recv()
+            over_plane[j] = dot(ungroup[...], z_recv[j]).astype(bf16)
+            plane_recv[j, in_plane, :] = over_plane[j, in_plane, :]
+            send_over_plane(j)
+
+    send_all()
+
+    pass_on(0)
 
     for load in loads[4:7]:
         load.wait()
@@ -240,8 +286,6 @@
     id_copy(0, other).start()
     lax.fori_loop(1, nplane, send_ids, 0, unroll=5)
 
-    pass_on(order[0])
-
     at_row = iota((rows, LANES), 0) == frow
     slot_of_row = jnp.sum(jnp.where(at_row, in_slot + 1.0, 0.0), axis=1, keepdims=True) - 1.0
     bolt[...] = jnp.broadcast_to(
@@ -251,52 +295,41 @@
     by_row = as_column(frow) == iota((LANES, rows), 1)
     slots_along = jnp.sum(jnp.where(by_row, as_column(in_slot) + 1.0, 0.0), axis=0, keepdims=True)
     bolts_along = jnp.sum(jnp.where(by_row, as_column(fstiff), 0.0), axis=0, keepdims=True)
-    joint_row = jnp.sum(
-        jnp.where(iota((jslots, njoint), 0) == jslot, joint_rows[...].astype(f32) + 1.0, 0.0),
-        axis=1, keepdims=True,
-    ) - 1.0
-    takes = joint_row == iota((jslots, rows), 1)
+    takes = as_column(joint_rows[...].astype(f32)) == iota((njoint, rows), 1)
     joint_select[...] = ones_where(takes)
     joint_slot = jnp.sum(jnp.where(takes, slots_along, 0.0), axis=1, keepdims=True) - 1.0
-    joint_flange[...] = ones_where(joint_slot == iota((jslots, fslots), 1))
+    joint_flange[...] = ones_where(joint_slot == iota((njoint, fslots), 1))
     joint_bolt[...] = jnp.broadcast_to(
         jnp.sum(jnp.where(takes, bolts_along, 0.0), axis=1, keepdims=True), joint_bolt.shape
     )
-
-    pass_on(order[1])
-    pass_on(order[2])
+    joint_place[...] = ones_where(iota((jslots, njoint), 0) == jslot)
 
     loads[7].wait()
     load_stiff.wait()
-    modes_copy.wait()
-
-    half_cols = cols // 2
-
-    def block_row(p):
+
+
+    def block_row(q):
         def run(r, carry):
             at = pl.ds(pl.multiple_of(r * BLOCK, BLOCK), BLOCK)
+            taken = jnp.concatenate([whole[q][block_cols[0, k, r]] for k in range(NEIGH)], axis=0)
+            own = whole[q][half * nblocks + r].astype(f32)
+            value = dot(stiff[at, :], taken)
             for e in range(2):
-                span = slice(e * cols + p * half_cols, e * cols + (p + 1) * half_cols)
-                two = slice(p * half_cols, (p + 1) * half_cols)
-                taken = jnp.concatenate(
-                    [whole[block_cols[0, k, r], :, span] for k in range(NEIGH)], axis=0
-                )
-                own = whole[half * nblocks + r, :, span].astype(f32)
-                value = dot(stiff[at, :], taken) + bolt[at, 0:1] * own
-                top = value.astype(bf16)
-                base[e, at, two] = value
-                high[e, at, two] = top
-                low[e, at, two] = (value - top.astype(f32)).astype(bf16)
+                span = slice(e * LANES, (e + 1) * LANES)
+                here_value = value[:, span] + bolt[at, :] * own[:, span]
+                top = here_value.astype(bf16)
+                base[e, q, at, :] = here_value
+                high[e, q, at, :] = top
+                low[e, q, at, :] = (here_value - top.astype(f32)).astype(bf16)
             return carry
 
         return run
 
-    def base_rows(p):
-        two = slice(p * half_cols, (p + 1) * half_cols)
-        for e in range(2):
-            joint_base[e, :, two] = dot(joint_select[...], high[e, :, two]) + dot(
-                joint_select[...], low[e, :, two]
-            )
+    def product(q):
+        modes_copies[q].wait()
+        lax.fori_loop(0, nblocks, block_row(q), 0, unroll=16)
+        sides = [jnp.concatenate([part[0, q], part[1, q]], axis=1) for part in (high, low)]
+        joint_base[q] = dot(joint_select[...], sides[0]) + dot(joint_select[...], sides[1])
 
     def rows_copy(k, e, jj, g):
         dest = lax.rem(plane + k, nplane)
@@ -327,30 +360,31 @@
         span = slice(jj * LANES, (jj + 1) * LANES)
         for e in range(2):
             j = e * quarter + jj
-            z_wait(j).wait_recv()
-            part = z_recv[j]
+            if jj < last:
+                z_wait(j).wait_recv()
+                part = z_recv[j]
+            else:
+                plane_wait(j).wait_recv()
+                part = dot(regroup[...], plane_recv[j]).astype(bf16)
             incoming[e, :, span] = part
-            rows_send[j] = (
-                joint_base[e, :, span] - joint_bolt[...] * dot(joint_flange[...], part)
+            entries = (
+                joint_base[jj, :, e * LANES : (e + 1) * LANES]
+                - joint_bolt[...] * dot(joint_flange[...], part)
             ).astype(bf16)
+            rows_send[j] = dot(joint_place[...], entries).astype(bf16)
             send_rows(e, jj, 0)
         for e in range(2):
             send_rows(e, jj, 1)
 
-    lax.fori_loop(0, nblocks // 2, block_row(0), 0)
-    pass_on(order[3])
-    lax.fori_loop(nblocks // 2, nblocks, block_row(0), 0)
-    pass_on(order[4])
-    pass_on(order[5])
-    base_rows(0)
+    product(0)
+    pass_on(1)
     joint_rows_out(0)
-    pass_on(order[6])
-    pass_on(order[7])
+    pass_on(2)
+    pass_on(3)
+    product(1)
     joint_rows_out(1)
-    lax.fori_loop(0, nblocks, block_row(1), 0)
-    base_rows(1)
+    product(2)
     joint_rows_out(2)
-    joint_rows_out(3)
 
     id_all = id_recv.at[pl.ds(0, 2 * (2 * nplane - 1))]
     id_wait = pltpu.make_async_remote_copy(
@@ -369,31 +403,8 @@
                 iota((NZ // 2 * JOWN, LANES), 0) == key
             )
 
-    step = 256
-
-    def round_rows(which, m):
-        at = pl.ds(pl.multiple_of(m * step, step), step)
-        partner = dot(select_row[at, :], incoming[which])
-        return (base[which, at, :] - bolt[at, 0:1] * partner).astype(bf16)
-
-    def round_other(m, carry):
-        round_send[pl.ds(pl.multiple_of(m * step, step), step), :] = round_rows(other, m)
-        return carry
-
-    def round_own(m, carry):
-        at = pl.ds(pl.multiple_of(half * rows + m * step, step), step)
-        round_full[at, :] = round_rows(half, m)
-        return carry
-
-    lax.fori_loop(0, rows // step, round_other, 0)
-    round_copy = pltpu.make_async_remote_copy(
-        round_send, round_full.at[own_rows], round_sem.at[0], round_sem.at[1], **to(comp, other)
-    )
-    round_copy.start()
-
     factor = 1.0 / math.sqrt(2 * rows)
     got_rows = pl.ds(0, (2 * nplane - 1) * unit)
-    width = iface // quarter
 
     def add_up(jj, g):
         landed = rows_recv.at[jj, g, got_rows]
@@ -418,29 +429,56 @@
             def _():
                 part_recv[jj, mine, :] = part_send[jj, g, rows_there, :]
 
-    def project(piece):
-        span = slice(piece * width, (piece + 1) * width)
-        reduced[0, span, :] = (
-            lax.dot_general(
-                whole[:, :, span].reshape(2 * rows, width), round_full[...], (((0,), (0,)), ((), ())),
-                preferred_element_type=f32,
+    def project(q):
+        full = lax.dot_general(
+            whole[q][...].reshape(2 * rows, 2 * LANES), round_full[...], (((0,), (0,)), ((), ())),
+            preferred_element_type=f32,
+        )
+        for e in range(2):
+            reduced[0, e * cols + q * LANES : e * cols + (q + 1) * LANES, :] = (
+                full[e * LANES : (e + 1) * LANES] * factor
             )
-            * factor
-        )
+
+    step = 256
+
+    def round_rows(which, m, target, first):
+        at = pl.ds(pl.multiple_of(m * step, step), step)
+        partner = dot(select_row[at, :], incoming[which])
+        for q in range(quarter):
+            span = slice(q * LANES, (q + 1) * LANES)
+            target[pl.ds(pl.multiple_of(first + m * step, step), step), span] = (
+                base[which, q, at, :] - bolt[at, :] * partner[:, span]
+            ).astype(bf16)
+
+    def round_other(m, carry):
+        round_rows(other, m, round_send, 0)
+        return carry
+
+    def round_own(m, carry):
+        round_rows(half, m, round_full, half * rows)
+        return carry
+
+    round_copy = pltpu.make_async_remote_copy(
+        round_send, round_full.at[own_rows], round_sem.at[0], round_sem.at[1], **to(comp, other)
+    )
 
     add_up(0, 0)
+    product(3)
+    joint_rows_out(3)
     add_up(0, 1)
-    lax.fori_loop(0, rows // step, round_own, 0)
     add_up(1, 0)
     add_up(1, 1)
+    lax.fori_loop(0, rows // step, round_other, 0)
+    round_copy.start()
+    add_up(2, 0)
+    lax.fori_loop(0, rows // step, round_own, 0)
+    add_up(2, 1)
     round_copy.wait()
     project(0)
+    add_up(3, 0)
     project(1)
-    add_up(2, 0)
-    add_up(2, 1)
+    add_up(3, 1)
     project(2)
-    add_up(3, 0)
-    add_up(3, 1)
     project(3)
 
     for jj in range(quarter):
@@ -453,7 +491,7 @@
             total = total + part_recv[jj, z * JOWN : (z + 1) * JOWN, :].astype(f32)
         forces[:, jj * LANES : (jj + 1) * LANES] = total
 
-    for j in order:
+    for j in range(chunks):
         plane_wait(j).wait_send()
         z_wait(j).wait_send()
     id_wait.wait_send()
@@ -470,6 +508,17 @@
         ).wait_send()
 
 
+def store(reduced, forces, reduced_hbm, forces_hbm, sem):
+    copies = [
+        pltpu.make_async_copy(reduced, reduced_hbm, sem.at[0]),
+        pltpu.make_async_copy(forces, forces_hbm, sem.at[1]),
+    ]
+    for copy in copies:
+        copy.start()
+    for copy in copies:
+        copy.wait()
+
+
 def body(*args):
     modes, stiff = args[0], args[1]
     ncomp = lax.axis_size("comp")
@@ -477,7 +526,7 @@
     cols = iface // 2
     quarter = cols // LANES
     chunks = 2 * quarter
-    width = stiff.shape[2]
+    width, njoint = stiff.shape[2], args[7].shape[1]
     fslots, jslots = ncomp * FCAP, ncomp * JCAP
     nplane = ncomp // NZ
     dma = pltpu.SemaphoreType.DMA
@@ -485,25 +534,27 @@
     hbm = pl.BlockSpec(memory_space=pl.ANY)
     scratch = [pltpu.SMEM((1, NEIGH, rows // BLOCK), jnp.int32)]
     scratch += [pltpu.VMEM(a.shape, a.dtype) for a in args[3:]]
+    scratch += [pltpu.VMEM((2 * rows // BLOCK, BLOCK, 2 * LANES), bf16)] * quarter
     scratch += [
-        pltpu.VMEM((2 * rows // BLOCK, BLOCK, iface), bf16),
         pltpu.VMEM((rows, width), bf16),
         pltpu.VMEM((8, LANES), f32),
         pltpu.VMEM((chunks, fslots, LANES), bf16),
         pltpu.VMEM((chunks, fslots, LANES), bf16),
         pltpu.VMEM((fslots, fslots), bf16),
+        pltpu.VMEM((fslots, fslots), bf16),
         pltpu.VMEM((chunks, fslots, LANES), bf16),
         pltpu.VMEM((chunks, fslots, LANES), bf16),
         pltpu.VMEM((2, fslots, cols), bf16),
-        pltpu.VMEM((2, rows, cols), f32),
-        pltpu.VMEM((2, rows, cols), bf16),
-        pltpu.VMEM((2, rows, cols), bf16),
+        pltpu.VMEM((2, quarter, rows, LANES), f32),
+        pltpu.VMEM((2, quarter, rows, LANES), bf16),
+        pltpu.VMEM((2, quarter, rows, LANES), bf16),
         pltpu.VMEM((rows, LANES), f32),
         pltpu.VMEM((rows, fslots), bf16),
-        pltpu.VMEM((jslots, rows), bf16),
-        pltpu.VMEM((jslots, fslots), bf16),
-        pltpu.VMEM((jslots, LANES), f32),
-        pltpu.VMEM((2, jslots, cols), f32),
+        pltpu.VMEM((njoint, rows), bf16),
+        pltpu.VMEM((njoint, fslots), bf16),
+        pltpu.VMEM((njoint, LANES), f32),
+        pltpu.VMEM((jslots, njoint), bf16),
+        pltpu.VMEM((quarter, njoint, 2 * LANES), f32),
         pltpu.VMEM((2 * nplane, 1, LANES), f32),
         pltpu.VMEM((4 * nplane, 1, LANES), f32),
         pltpu.VMEM((2, NZ // 2 * JOWN, jslots), bf16),
@@ -513,11 +564,11 @@
         pltpu.VMEM((2 * rows, cols), bf16),
         pltpu.VMEM((quarter, 2, NZ // 2 * JOWN, LANES), bf16),
         pltpu.VMEM((quarter, NZ * JOWN, LANES), bf16),
-        dma((2,)), dma((8,)), dma, dma((chunks,)), dma, dma((chunks,)),
-        dma((2,)), dma((2,)), dma, dma((chunks,)),
+        dma((chunks + 1,)), dma((8,)), dma, dma((chunks,)), dma, dma((chunks,)),
+        dma((2, quarter)), dma((2,)), dma, dma((chunks,)),
         dma((2,)), dma, dma((quarter,)),
     ]
-    return pl.pallas_call(
+    results = pl.pallas_call(
         kernel,
         out_shape=(
             pltpu.VMEM((1, iface, cols), f32),
@@ -530,6 +581,13 @@
             collective_id=0, has_side_effects=True, vmem_limit_bytes=56 << 20
         ),
     )(modes.reshape(rows // BLOCK, BLOCK, iface), stiff, jnp.swapaxes(args[2], 1, 2), *args[3:])
+    return pl.pallas_call(
+        store,
+        out_shape=tuple(jax.ShapeDtypeStruct(r.shape, r.dtype) for r in results),
+        in_specs=[vmem, vmem],
+        out_specs=(hbm, hbm),
+        scratch_shapes=[dma((2,))],
+    )(*(pltpu.with_memory_space_constraint(r, pltpu.VMEM) for r in results))
 
 
 def solution(mesh):

time: 48.9 us -> 46.1 us (0.943)
  local copies, waits for them, and re-layouts: 1.98 us -> 0 us
  Pallas kernels: 46.2 us -> 45.4 us
    pallas_call x1, Pallas kernels: 46.2 us -> 44 us  [body(): pl.pallas_call(kernel, out_shape=(pltpu.VMEM((1, iface, cols), f32), pltp...]
    unnamed x2 -> x0, local copies, waits for them, and re-layouts: 1.98 us -> none
    pallas_call x0 -> x1, Pallas kernels: none -> 1.36 us  [body(): pl.pallas_call(store, out_shape=tuple((jax.ShapeDtypeStruct(r.shape, r.dt...]
where the time goes in v3:
time: 46.1 us; the launch traced here: 46 us
  Pallas kernels  45.4 us (98%)
  between operations  0.64 us (1%)
    pallas_call x1, Pallas kernels, body(): pl.pallas_call(kernel, out_shape=(pltpu.VMEM((1, iface, cols), f32), pltp...  44 us
    pallas_call x1, Pallas kernels, body(): pl.pallas_call(store, out_shape=tuple((jax.ShapeDtypeStruct(r.shape, r.dt...  1.36 us

profile of v3, /device:TPU:1, one launch (start us, length us, event | category | flops | bytes accessed | tf_op | source)
XLA Modules:
  0.0 46.0 jit_solution(5905998904849239242)
XLA Ops:
  0.6 44.0 %shard_map.113 = (f32[1,1024,512]{2,1,0:T(8,128)S(1)}, f32[64,512]{1,0:T(8,128)S(1)}) custom-call(bf16[16,64,1024]{2,1,0:T(8,128)(2,1)} %bitcast.2, bf16[1,1024,512]{2,1,0:T(8,128)(2,1)} %stiff_hbm.1, s32[1,8,16]{2,1,0:T(8,128)} %bitcast.3, s32[1,126]{1,0:T(1,128)} %flange_rows_hbm.1, s32[1,126]{1,0:T(1,128)} %flange_dest_hbm.1, s32[1,126]{1,0:T(1,128)} %flange_match_hbm.1, ...), custom_call_target="tpu_custom_call" | custom-call | tf_op jit(solution)/shard_map/pallas_call | solution.py:571
  44.6 1.4 %shard_map.114 = (f32[1,1024,512]{2,1,0:T(8,128)}, f32[64,512]{1,0:T(8,128)}) custom-call(f32[1,1024,512]{2,1,0:T(8,128)S(1)} %get-tuple-element.4.reduced, f32[64,512]{1,0:T(8,128)S(1)} %get-tuple-element.5.forces), custom_call_target="tpu_custom_call" | custom-call | tf_op jit(solution)/shard_map/pallas_call | solution.py:584

commit v4 on v3

--- a/solution.py
+++ b/solution.py
@@ -121,7 +121,7 @@
         return carry
 
     lax.fori_loop(1, NZ, greet_z, 0, unroll=7)
-    lax.fori_loop(1, nplane, greet_plane, 0, unroll=5)
+    lax.fori_loop(1, nplane, greet_plane, 0, unroll=15)
     pl.semaphore_signal(barrier, inc=1, **to(comp, other))
 
     for load in loads[:4]:
@@ -172,7 +172,7 @@
             ).start()
             return carry
 
-        lax.fori_loop(1, nplane, send, 0, unroll=5)
+        lax.fori_loop(1, nplane, send, 0, unroll=15)
 
     gather(0)
 
@@ -284,7 +284,7 @@
         return carry
 
     id_copy(0, other).start()
-    lax.fori_loop(1, nplane, send_ids, 0, unroll=5)
+    lax.fori_loop(1, nplane, send_ids, 0, unroll=15)
 
     at_row = iota((rows, LANES), 0) == frow
     slot_of_row = jnp.sum(jnp.where(at_row, in_slot + 1.0, 0.0), axis=1, keepdims=True) - 1.0
@@ -344,7 +344,7 @@
             rows_copy(k, e, jj, g).start()
             return carry
 
-        lax.fori_loop(1, nplane, send, 0, unroll=5)
+        lax.fori_loop(1, nplane, send, 0, unroll=15)
 
         @pl.when(half != e)
         def _():
@@ -384,7 +384,6 @@
     product(1)
     joint_rows_out(1)
     product(2)
-    joint_rows_out(2)
 
     id_all = id_recv.at[pl.ds(0, 2 * (2 * nplane - 1))]
     id_wait = pltpu.make_async_remote_copy(
@@ -463,9 +462,10 @@
     )
 
     add_up(0, 0)
+    add_up(0, 1)
+    joint_rows_out(2)
     product(3)
     joint_rows_out(3)
-    add_up(0, 1)
     add_up(1, 0)
     add_up(1, 1)
     lax.fori_loop(0, rows // step, round_other, 0)

time: 46.1 us -> 45.4 us (0.985)
  Pallas kernels: 45.4 us -> 44.5 us
    pallas_call x1, Pallas kernels: 44 us -> 43.2 us  [body(): pl.pallas_call(kernel, out_shape=(pltpu.VMEM((1, iface, cols), f32), pltp...]
where the time goes in v4:
time: 45.4 us; the launch traced here: 45.3 us
  Pallas kernels  44.5 us (98%)
  between operations  0.8 us (2%)
    pallas_call x1, Pallas kernels, body(): pl.pallas_call(kernel, out_shape=(pltpu.VMEM((1, iface, cols), f32), pltp...  43.2 us
    pallas_call x1, Pallas kernels, body(): pl.pallas_call(store, out_shape=tuple((jax.ShapeDtypeStruct(r.shape, r.dt...  1.36 us

profile of v4, /device:TPU:1, one launch (start us, length us, event | category | flops | bytes accessed | tf_op | source)
XLA Modules:
  0.0 45.3 jit_solution(5620596771876903066)
XLA Ops:
  0.6 43.2 %shard_map.113 = (f32[1,1024,512]{2,1,0:T(8,128)S(1)}, f32[64,512]{1,0:T(8,128)S(1)}) custom-call(bf16[16,64,1024]{2,1,0:T(8,128)(2,1)} %bitcast.2, bf16[1,1024,512]{2,1,0:T(8,128)(2,1)} %stiff_hbm.1, s32[1,8,16]{2,1,0:T(8,128)} %bitcast.3, s32[1,126]{1,0:T(1,128)} %flange_rows_hbm.1, s32[1,126]{1,0:T(1,128)} %flange_dest_hbm.1, s32[1,126]{1,0:T(1,128)} %flange_match_hbm.1, ...), custom_call_target="tpu_custom_call" | custom-call | tf_op jit(solution)/shard_map/pallas_call | solution.py:571
  43.8 1.4 %shard_map.114 = (f32[1,1024,512]{2,1,0:T(8,128)}, f32[64,512]{1,0:T(8,128)}) custom-call(f32[1,1024,512]{2,1,0:T(8,128)S(1)} %get-tuple-element.4.reduced, f32[64,512]{1,0:T(8,128)S(1)} %get-tuple-element.5.forces), custom_call_target="tpu_custom_call" | custom-call | tf_op jit(solution)/shard_map/pallas_call | solution.py:584

commit v5 on v4

--- a/solution.py
+++ b/solution.py
@@ -136,10 +136,8 @@
     ).astype(f32)
     vec[3:4, 0:nflange] = flange_stiff[...]
     frow, out_slot, in_slot, fstiff = vec[0:1, :], vec[1:2, :], vec[2:3, :], vec[3:4, :]
-    row_of_slot = jnp.sum(
-        jnp.where(iota((fslots, LANES), 0) == out_slot, frow + 1.0, 0.0), axis=1, keepdims=True
-    ) - 1.0
-    pick = ones_where(row_of_slot == iota((fslots, rows), 1))
+    pick = ones_where(as_column(frow) == iota((LANES, rows), 1))
+    into_slot = ones_where(iota((fslots, LANES), 0) == out_slot)
     last = quarter - 1
     pair = NZ * FCAP
     line = nplane * FCAP
@@ -155,7 +153,8 @@
     def gather(q):
         for load in load_modes[q]:
             load.wait()
-        got = dot(pick, whole[q][own_blocks].reshape(rows, 2 * LANES))
+        nodes = dot(pick, whole[q][own_blocks].reshape(rows, 2 * LANES)).astype(bf16)
+        got = dot(into_slot, nodes)
         for e in range(2):
             j = e * quarter + q
             over_plane[j] = got[:, e * LANES : (e + 1) * LANES].astype(bf16)

time: 45.4 us -> 45.5 us (level)
  no operation moved by 1% of the time
where the time goes in v5:
time: 45.5 us; the launch traced here: 45.3 us
  Pallas kernels  44.5 us (98%)
  between operations  0.8 us (2%)
    pallas_call x1, Pallas kernels, body(): pl.pallas_call(kernel, out_shape=(pltpu.VMEM((1, iface, cols), f32), pltp...  43.1 us
    pallas_call x1, Pallas kernels, body(): pl.pallas_call(store, out_shape=tuple((jax.ShapeDtypeStruct(r.shape, r.dt...  1.36 us

profile of v5, /device:TPU:1, one launch (start us, length us, event | category | flops | bytes accessed | tf_op | source)
XLA Modules:
  0.0 45.3 jit_solution(16861490101352320528)
XLA Ops:
  0.6 43.1 %shard_map.113 = (f32[1,1024,512]{2,1,0:T(8,128)S(1)}, f32[64,512]{1,0:T(8,128)S(1)}) custom-call(bf16[16,64,1024]{2,1,0:T(8,128)(2,1)} %bitcast.2, bf16[1,1024,512]{2,1,0:T(8,128)(2,1)} %stiff_hbm.1, s32[1,8,16]{2,1,0:T(8,128)} %bitcast.3, s32[1,126]{1,0:T(1,128)} %flange_rows_hbm.1, s32[1,126]{1,0:T(1,128)} %flange_dest_hbm.1, s32[1,126]{1,0:T(1,128)} %flange_match_hbm.1, ...), custom_call_target="tpu_custom_call" | custom-call | tf_op jit(solution)/shard_map/pallas_call | solution.py:570
  43.8 1.4 %shard_map.114 = (f32[1,1024,512]{2,1,0:T(8,128)}, f32[64,512]{1,0:T(8,128)}) custom-call(f32[1,1024,512]{2,1,0:T(8,128)S(1)} %get-tuple-element.4.reduced, f32[64,512]{1,0:T(8,128)S(1)} %get-tuple-element.5.forces), custom_call_target="tpu_custom_call" | custom-call | tf_op jit(solution)/shard_map/pallas_call | solution.py:583
